TPU v7x, 32 devices: a whole 2x2x4 slice. The times are simulated.
32 devices in a mesh: exp: 8 (over y, x, core), imp: 4 (over z).
Axes of the slice: x: 2, y: 2, z: 4, core: 2. Of those that a mesh axis runs over, the one named last changes fastest.
Arguments:
- flows: bfloat16 [128, 256, 256], P(('exp', 'imp')), may hold values from 0 to 8, as said below
- routing: int32 [32, 4, 1], P(('exp', 'imp')), may hold values from -1 to 3, as said below
- tile_block: int32 [128], P(('exp', 'imp')), may hold values from 0 to 7, as said below
- exp_country: int32 [4096], P('exp'), may hold values from 0 to 127, never falling along the last dimension, each value on 1 to 64 neighbouring positions
- imp_country: int32 [4096], P('imp'), may hold values from 0 to 127, never falling along the last dimension, each value on 1 to 64 neighbouring positions
Outputs:
- exporter_effects: float32 [4096], P('exp')
- importer_effects: float32 [4096], P('imp')
- pair_effects: float32 [128, 128], replicated
Inputs may be any that keep to these rules, and one draw needn't show every extreme that they name: `routing`: entry [d, t, s] names a slot of device d routed to imp index t, or is -1. Each slot is named at most once. The devices of one exp index route at most 3 named slots to each imp index in all, and exactly 3 to some imp index of every exp index; each entry names at most one slot, and some entry of some device does name one; in every exp index some device names all 4 of its slots. `tile_block`: r * 4 + c for the slot's local exporter block r and local importer block c; distinct within a device. `exp_country`: never falls along the exporter-years; every country has 1 to 64 of them. `imp_country`: never falls along the importer-years; every country has 1 to 64 of them. Positive flows.
All inputs are finite; a program needn't handle non-finite values.
Results may differ from a plain program's by a relative error of at most 0.0003.
Values may be sent and summed in bfloat16 or wider, within the bound.
No kernel may reach another device: no remote copies, remote signals or barrier semaphores. Data moves between devices by JAX's collectives and lax.ppermute only.
A program may use at most 64 MiB of HBM per device.

v0:
```python
import functools

import jax
import jax.numpy as jnp
from jax import lax
from jax.experimental import pallas as pl
from jax.experimental.pallas import tpu as pltpu
from jax.sharding import PartitionSpec as P

NCE = 128
NCI = 128
NEWTON = 2
CG = 2
LANES = 128
RIDGE = 64.0
VMEM_BYTES = 48 * 1024 * 1024
LOCAL_BYTES = 56 * 1024 * 1024

f32 = jnp.float32
bf16 = jnp.bfloat16
i32 = jnp.int32


def iota(shape, dim):
    return lax.broadcasted_iota(i32, shape, dim)


def split(x):
    hi = x.astype(bf16).astype(f32)
    rest = x - hi
    mid = rest.astype(bf16).astype(f32)
    return hi, mid, rest - mid


def dot(x, y, cx, cy, precision=None):
    return lax.dot_general(
        x, y, (((cx,), (cy,)), ((), ())), precision=precision, preferred_element_type=f32
    )


class Layout:
    def __init__(self, na, nb, side):
        self.na, self.nb, self.side = na, nb, side
        self.rows_at = NCE
        self.cols_at = self.rows_at + na // LANES
        self.cnt_at = self.cols_at + nb // LANES
        self.live_at = self.cnt_at + 2
        self.blocks_a, self.blocks_b = na // side, nb // side
        self.total = -(-(self.live_at - (-self.blocks_a * self.blocks_b // LANES)) // 8) * 8
        self.share = -(-self.total // 16) * 8


def half_of(exp_place, imp_place):
    bits = exp_place ^ imp_place
    for shift in (8, 4, 2, 1):
        bits = bits ^ (bits >> shift)
    return bits & 1


def local_kernel(lay, slots, *refs):
    sources, outs, out, homes, sems = refs[:5], refs[5:7], refs[7], refs[8:13], refs[13]
    copies = [pltpu.make_async_copy(x, y, sems.at[j]) for j, (x, y) in enumerate(zip(sources, homes))]
    for copy in copies:
        copy.start()
    flows, routing, tile_block, ec, ic = homes
    exp_place, imp_place = lax.axis_index("exp"), lax.axis_index("imp")
    side = lay.side
    row_blocks = ec.shape[0]
    col_local = ic.shape[0]
    out[...] = jnp.zeros_like(out)
    per = side // LANES
    country = iota((NCE, side), 0)
    ones = jnp.ones((8, side), bf16)
    for copy in copies:
        copy.wait()
    pairs = jnp.zeros((NCE, NCI), f32)
    for k in range(slots):
        r = tile_block[k] // col_local
        c = tile_block[k] % col_local
        live = routing[0] == k
        for t in range(1, routing.shape[0]):
            live = live | (routing[t] == k)
        keep = live.astype(f32)
        hot_r = (country == ec[r]).astype(f32).astype(bf16)
        hot_c = (country == ic[c]).astype(f32).astype(bf16)
        tile = flows[k] * keep.astype(bf16)
        half = dot(hot_r, tile, 1, 0)
        col_sum = jnp.sum(half, axis=0, keepdims=True)
        row_sum = dot(ones, tile, 1, 1)[0:1]
        for piece in split(half):
            pairs = pairs + dot(piece.astype(bf16), hot_c, 1, 1)
        row_at = lay.rows_at + (exp_place * row_blocks + r) * per
        col_at = lay.cols_at + (imp_place * col_local + c) * per
        for h in range(per):
            cut = slice(h * LANES, (h + 1) * LANES)
            out[pl.ds(row_at + h, 1), :] += row_sum[:, cut]
            out[pl.ds(col_at + h, 1), :] += col_sum[:, cut]
        flat = (exp_place * row_blocks + r) * lay.blocks_b + imp_place * col_local + c
        here = iota((1, LANES), 1) == flat % LANES
        out[pl.ds(lay.live_at + flat // LANES, 1), :] += jnp.where(here, keep, 0.0)
    out[0:NCE, :] = pairs
    cnt_a = jnp.zeros((8, LANES), f32)
    for r in range(row_blocks):
        cnt_a += dot(ones, (country == ec[r]).astype(f32).astype(bf16), 1, 1)
    cnt_b = jnp.zeros((8, LANES), f32)
    for c in range(col_local):
        cnt_b += dot(ones, (country == ic[c]).astype(f32).astype(bf16), 1, 1)
    cnt_a = cnt_a[0:1] * (imp_place == 0).astype(f32)
    cnt_b = cnt_b[0:1] * (exp_place == 0).astype(f32)
    out[lay.cnt_at : lay.cnt_at + 1, :] = cnt_a
    out[lay.cnt_at + 1 : lay.cnt_at + 2, :] = cnt_b
    mine = half_of(exp_place, imp_place)
    for k, part in enumerate(outs):
        part[...] = out[pl.ds(pl.multiple_of((mine ^ k) * lay.share, 8), lay.share), :]


def lookup(row, index):
    return jnp.take_along_axis(
        jnp.broadcast_to(row, index.shape), index, axis=1, mode="promise_in_bounds"
    )


def down(row):
    return jnp.transpose(jnp.broadcast_to(row, (LANES, LANES)))


def across(x):
    return jnp.sum(jnp.transpose(x), axis=0, keepdims=True)


def below(x):
    return jnp.sum(x, axis=0, keepdims=True)


def eights(x):
    return functools.reduce(lambda u, v: u + v, [x[j : j + 8] for j in range(0, x.shape[0], 8)])


def inner(u, v):
    partial = eights(u[0] * v[0]) + eights(u[1] * v[1]) + eights(u[2] * v[2])
    return jnp.sum(below(partial), axis=1, keepdims=True)


class Side:
    def __init__(self, n, block, start, middle, end, hot, stage):
        self.n, self.block, self.hot, self.stage = n, block, hot, stage
        self.chunks = n // LANES
        shape = (self.chunks, LANES)
        place = (iota(shape, 0) * LANES + iota(shape, 1)).astype(f32)
        country = jnp.zeros(shape, i32)
        jump = LANES // 2
        while jump:
            passed = lookup(end, country + (jump - 1)) <= place
            country = jnp.where(passed, country + jump, country)
            jump //= 2
        self.country = country
        self.second = place >= lookup(middle, country)
        for j in range(n // block):
            at = (iota((block, LANES), 0) + j * block).astype(f32)
            inside = (at >= start) & (at < end)
            hot[j * block : (j + 1) * block, :] = jnp.where(inside, 1.0, 0.0).astype(bf16)

    def expand(self, first, second):
        return jnp.where(self.second, lookup(second, self.country), lookup(first, self.country))

    def sums(self, vectors):
        chunks, stage = self.chunks, self.stage
        for k, v in enumerate(vectors):
            stage[2 * k * chunks : (2 * k + 1) * chunks, :] = jnp.where(self.second, 0.0, v)
            stage[(2 * k + 1) * chunks : (2 * k + 2) * chunks, :] = jnp.where(self.second, v, 0.0)
        high = -(-2 * len(vectors) // 8) * 8
        for k in range(2 * len(vectors), high):
            stage[k * chunks : (k + 1) * chunks, :] = jnp.zeros((chunks, LANES), f32)
        got = jnp.zeros((3 * high, LANES), f32)
        per = self.block // LANES
        for j in range(chunks // per):
            left = jnp.concatenate(
                [stage[pl.ds(j * per + h, high, stride=chunks), :] for h in range(per)], axis=1
            )
            pieces = jnp.concatenate(split(left), axis=0).astype(bf16)
            got += dot(pieces, self.hot[j * self.block : (j + 1) * self.block, :], 1, 0)
        return got[:high] + got[high : 2 * high] + got[2 * high :]

    def maxima(self, values_ref, low, high):
        low, high = down(low), down(high)

        def body(j, best):
            at = (iota((LANES, LANES), 1) + j * LANES).astype(f32)
            inside = (at >= low) & (at < high)
            return jnp.maximum(best, jnp.where(inside, values_ref[pl.ds(j, 1), :], -jnp.inf))

        best = lax.fori_loop(0, self.chunks, body, jnp.full((LANES, LANES), -jnp.inf, f32))
        best = jnp.max(jnp.transpose(best), axis=0, keepdims=True)
        return jnp.where(best > -jnp.inf, best, 0.0)


def solve_kernel(lay, *refs):
    where = lax.axis_index("exp"), lax.axis_index("imp")
    shares, refs = refs[:2], refs[2:]
    out_a, out_b, out_g, shared, hot_a, hot_b, stage_a, stage_b, val_a, val_b, shift_ref = refs
    mine = half_of(*where)
    for k, part in enumerate(shares):
        shared[pl.ds(pl.multiple_of((mine ^ k) * lay.share, 8), lay.share), :] = part[...]
    flow = (
        shared[lay.rows_at : lay.cols_at, :],
        shared[lay.cols_at : lay.cnt_at, :],
        shared[0:NCE, :],
    )
    side = lay.side
    tally = shared[lay.cnt_at : lay.cnt_at + 8, :]
    before = jnp.where(iota((LANES, LANES), 0) < iota((LANES, LANES), 1), 1.0, 0.0).astype(bf16)
    start = dot(tally.astype(bf16), before, 1, 0)
    end = start + tally
    first = jnp.floor((start + 0.5) * (1.0 / side))
    middle = jnp.minimum(end, (first + 1.0) * side)

    def table(x, y):
        return jnp.concatenate([x[0:1], y[0:1], x[1:2], y[1:2]], axis=0)

    low, high = table(start, middle), table(middle, end)
    count = high - low
    full = count > 0.5
    inv_count = jnp.where(full, 1.0 / jnp.maximum(count, 1.0), 0.0)
    block_of = jnp.where(full, table(first, first + 1.0), -1.0)
    sa = Side(lay.na, side, start[0:1], middle[0:1], end[0:1], hot_a, stage_a)
    sb = Side(lay.nb, side, start[1:2], middle[1:2], end[1:2], hot_b, stage_b)

    wide = lay.blocks_b
    spots = [(r * wide // LANES, r * wide % LANES) for r in range(lay.blocks_a)]
    live = jnp.concatenate(
        [shared[lay.live_at + row : lay.live_at + row + 1, at : at + wide] for row, at in spots], axis=0
    ).astype(bf16)
    number = iota((LANES, LANES), 1).astype(f32)
    pick_a = [jnp.where(down(block_of[p : p + 1]) == number, 1.0, 0.0).astype(bf16) for p in (0, 1)]
    number = iota((LANES, LANES), 0).astype(f32)
    pick_b = [jnp.where(block_of[q : q + 1] == number, 1.0, 0.0).astype(bf16) for q in (2, 3)]
    reach = [dot(pick[:, : lay.blocks_a], live, 1, 0).astype(bf16) for pick in pick_a]
    mask = [[dot(reach[p], pick_b[q][: lay.blocks_b], 1, 0) for q in (0, 1)] for p in (0, 1)]

    a = jnp.zeros((lay.na // LANES, LANES), f32)
    b = jnp.zeros((lay.nb // LANES, LANES), f32)
    g = jnp.zeros((NCE, NCI), f32)
    mean = jnp.zeros((4, LANES), f32)
    for newton in range(NEWTON):
        if newton == 0:
            left = flow
            weight, inv, rate = count, inv_count, mask
            sum_a, sum_b = sa.sums([flow[0]]), sb.sums([flow[1]])
            part_a, part_b = sa.expand(inv[0:1], inv[1:2]), sb.expand(inv[2:3], inv[3:4])
            m2, m3 = inv, inv * inv
            f1 = jnp.concatenate([sum_a[0:2], sum_b[0:2]], axis=0) * inv
            f2 = f1 * inv
        else:
            left = (flow[0] - RIDGE * a, flow[1] - RIDGE * b, flow[2] - RIDGE * g)
            shift_ref[0:4, :] = mean
            off_a = a - sa.expand(mean[0:1], mean[1:2])
            off_b = b - sb.expand(mean[2:3], mean[3:4])
            worst = jnp.maximum(jnp.max(off_a), jnp.max(off_b))
            val_a[...] = a
            val_b[...] = b

            @pl.when(worst > 20.0)
            def _():
                shift_ref[0:1, :] = sa.maxima(val_a, low[0:1], high[0:1])
                shift_ref[1:2, :] = sa.maxima(val_a, low[1:2], high[1:2])
                shift_ref[2:3, :] = sb.maxima(val_b, low[2:3], high[2:3])
                shift_ref[3:4, :] = sb.maxima(val_b, low[3:4], high[3:4])

            shift = shift_ref[0:4, :]
            size_a = jnp.exp(a - sa.expand(shift[0:1], shift[1:2]))
            size_b = jnp.exp(b - sb.expand(shift[2:3], shift[3:4]))

            def moments(s, x, f):
                return s.sums([x, x * x, x * x * x, x * f, x * x * f])

            sum_a, sum_b = moments(sa, size_a, left[0]), moments(sb, size_b, left[1])
            got = [jnp.concatenate([sum_a[2 * k : 2 * k + 2], sum_b[2 * k : 2 * k + 2]], axis=0) for k in range(5)]
            weight = got[0]
            inv = jnp.where(full, 1.0 / jnp.where(full, weight, 1.0), 0.0)
            part_a = size_a * sa.expand(inv[0:1], inv[1:2])
            part_b = size_b * sb.expand(inv[2:3], inv[3:4])
            inv2 = inv * inv
            m2, m3 = got[1] * inv2, got[2] * (inv2 * inv)
            f1, f2 = got[3] * inv, got[4] * inv2
            lift = [g + down(shift[p : p + 1]) for p in (0, 1)]
            rate = [
                [jnp.where(mask[p][q] > 0.5, jnp.exp(lift[p] + shift[2 + q : 3 + q]), 0.0) for q in (0, 1)]
                for p in (0, 1)
            ]
        tall = [down(weight[p : p + 1]) for p in (0, 1)]
        mu = [[rate[p][q] * (tall[p] * weight[2 + q : 3 + q]) for q in (0, 1)] for p in (0, 1)]
        mu_a = [mu[p][0] + mu[p][1] for p in (0, 1)]
        mu_b = [mu[0][q] + mu[1][q] for q in (0, 1)]
        whole = jnp.concatenate([across(mu_a[0]), across(mu_a[1]), below(mu_b[0]), below(mu_b[1])], axis=0)
        da = part_a * sa.expand(whole[0:1], whole[1:2])
        db = part_b * sb.expand(whole[2:3], whole[3:4])
        res = (left[0] - da, left[1] - db, left[2] - (mu_a[0] + mu_a[1]))
        way = res
        norm = inner(res, res)
        v = f1 - whole * m2
        w = f2 - whole * m3
        for sweep in range(CG):
            tall = [down(v[p : p + 1]) for p in (0, 1)]
            flat = [v[2 + q : 3 + q] for q in (0, 1)]
            ga = [mu[p][0] * flat[0] + mu[p][1] * flat[1] + way[2] * mu_a[p] for p in (0, 1)]
            gb = [mu[0][q] * tall[0] + mu[1][q] * tall[1] + way[2] * mu_b[q] for q in (0, 1)]
            u = jnp.concatenate([across(ga[0]), across(ga[1]), below(gb[0]), below(gb[1])], axis=0)
            image = (
                (da + RIDGE) * way[0] + part_a * sa.expand(u[0:1], u[1:2]),
                (db + RIDGE) * way[1] + part_b * sb.expand(u[2:3], u[3:4]),
                RIDGE * way[2] + (ga[0] + ga[1]) + (tall[0] * mu_a[0] + tall[1] * mu_a[1]),
            )
            step = norm / inner(way, image)
            a, b, g = a + step * way[0], b + step * way[1], g + step * way[2]
            if newton + 1 < NEWTON:
                mean = mean + step * v
            if sweep + 1 < CG:
                res = tuple(x - step * y for x, y in zip(res, image))
                fresh = inner(res, res)
                ratio = fresh / norm
                way = tuple(x + ratio * y for x, y in zip(res, way))
                norm = fresh
                v = v - step * (whole * w + RIDGE * v + u * m2) + ratio * v
    out_g[...] = g
    val_a[...] = a
    val_b[...] = b
    for out, val, at in ((out_a, val_a, where[0]), (out_b, val_b, where[1])):
        rows = out.shape[0] // LANES
        for j in range(rows):
            out[j * LANES : (j + 1) * LANES] = val[pl.ds(at * rows + j, 1), :].reshape(LANES)


def powers(first, limit):
    return [1 << k for k in range(16) if first <= 1 << k < limit]


def swap(x, n_exp, n_imp, exp_bits, imp_bits):
    pairs = [
        (e * n_imp + m, (e ^ exp_bits) * n_imp + (m ^ imp_bits)) for e in range(n_exp) for m in range(n_imp)
    ]
    return lax.ppermute(x, ("exp", "imp"), pairs)


def per_device(mesh_shape, flows, routing, tile_block, exp_country, imp_country):
    slots, side = flows.shape[0], flows.shape[1]
    n_exp, n_imp = mesh_shape
    rows, cols = exp_country.shape[0], imp_country.shape[0]
    lay = Layout(rows * n_exp, cols * n_imp, side)
    vmem = pl.BlockSpec(memory_space=pltpu.VMEM)
    inputs = (
        flows,
        routing.reshape(-1),
        tile_block,
        exp_country.reshape(-1, 1, side),
        imp_country.reshape(-1, 1, side),
    )
    homes = [pltpu.VMEM, pltpu.SMEM, pltpu.SMEM, pltpu.VMEM, pltpu.VMEM]
    parts = pl.pallas_call(
        functools.partial(local_kernel, lay, slots),
        out_shape=[jax.ShapeDtypeStruct((lay.share, LANES), f32)] * 2,
        in_specs=[pl.BlockSpec(memory_space=pltpu.HBM)] * 5,
        out_specs=[vmem] * 2,
        scratch_shapes=[pltpu.VMEM((2 * lay.share, LANES), f32)]
        + [space(x.shape, x.dtype) for space, x in zip(homes, inputs)]
        + [pltpu.SemaphoreType.DMA((5,))],
        compiler_params=pltpu.CompilerParams(vmem_limit_bytes=LOCAL_BYTES),
        name="local_sums",
    )(*inputs)
    mine = parts[0] + swap(parts[1], n_exp, n_imp, 1, 0)
    for bit in powers(2, n_exp):
        mine = mine + swap(mine, n_exp, n_imp, bit | 1, 0)
    for bit in powers(1, n_imp):
        mine = mine + swap(mine, n_exp, n_imp, 1, bit)
    shares = (mine, swap(mine, n_exp, n_imp, 1, 0))
    high = 16
    a, b, g = pl.pallas_call(
        functools.partial(solve_kernel, lay),
        out_shape=(
            jax.ShapeDtypeStruct((rows,), f32),
            jax.ShapeDtypeStruct((cols,), f32),
            jax.ShapeDtypeStruct((NCE, NCI), f32),
        ),
        in_specs=[vmem] * 2,
        out_specs=(vmem, vmem, vmem),
        scratch_shapes=[
            pltpu.VMEM((2 * lay.share, LANES), f32),
            pltpu.VMEM((lay.na, LANES), bf16),
            pltpu.VMEM((lay.nb, LANES), bf16),
            pltpu.VMEM((high * lay.na // LANES, LANES), f32),
            pltpu.VMEM((high * lay.nb // LANES, LANES), f32),
            pltpu.VMEM((lay.na // LANES, LANES), f32),
            pltpu.VMEM((lay.nb // LANES, LANES), f32),
            pltpu.VMEM((8, LANES), f32),
        ],
        compiler_params=pltpu.CompilerParams(vmem_limit_bytes=VMEM_BYTES),
        name="solve",
    )(*shares)
    return a, b, g


def solution(mesh):
    placed = (
        P(("exp", "imp"), None, None),
        P(("exp", "imp"), None, None),
        P(("exp", "imp")),
        P("exp"),
        P("imp"),
    )
    return jax.shard_map(
        functools.partial(per_device, (mesh.shape["exp"], mesh.shape["imp"])),
        mesh=mesh,
        in_specs=placed,
        out_specs=(P("exp"), P("imp"), P()),
        check_vma=False,
    )
```

profile of v0, /device:TPU:25, one launch (start us, length us, event | category | flops | bytes accessed | tf_op | source)
XLA Modules:
  0.0 30.1 jit_solution(9116924777005680378)
XLA Ops:
  0.6 2.7 %local_sums.1 = (f32[104,128]{1,0:T(8,128)}, f32[104,128]{1,0:T(8,128)}) custom-call(bf16[4,256,256]{2,1,0:T(8,128)(2,1)} %refs_0_.1, s32[4]{0:T(128)} %bitcast.5, s32[4]{0:T(128)} %refs_2_.1, s32[2,1,256]{2,1,0:T(1,128)} %bitcast.4, s32[4,1,256]{2,1,0:T(1,128)} %bitcast.3), custom_call_target="tpu_custom_call" | custom-call | tf_op jit(solution)/shard_map/local_sums/pallas_call | solution.py:358
  3.3 0.7 %collective-permute-start = (f32[104,128]{1,0:T(8,128)}, f32[104,128]{1,0:T(8,128)S(1)}, u32[]{:S(2)}, u32[]{:S(2)}) collective-permute-start(f32[104,128]{1,0:T(8,128)} %get-tuple-element.6), channel_id=1, source_target_pairs={{0,4},{1,5},{2,6},{3,7},{4,0},{5,1},{6,2},{7,3},{8,12},{9,13},{10,... | collective-permute-start | bytes 159752 | tf_op jit(solution)/shard_map/ppermute | solution.py:341
  4.0 1.1 %collective-permute-done = f32[104,128]{1,0:T(8,128)S(1)} collective-permute-done((f32[104,128]{1,0:T(8,128)}, f32[104,128]{1,0:T(8,128)S(1)}, u32[]{:S(2)}, u32[]{:S(2)}) %collective-permute-start) | collective-permute-done | bytes 53280 | tf_op jit(solution)/shard_map/ppermute | solution.py:341
  5.1 0.8 %add.15 = f32[104,128]{1,0:T(8,128)S(1)} add(f32[104,128]{1,0:T(8,128)} %get-tuple-element.5, f32[104,128]{1,0:T(8,128)S(1)} %collective-permute-done) | non-fusion elementwise | flops 13312 | bytes 159744 | tf_op jit(solution)/shard_map/add | solution.py:369
  5.9 1.5 %collective-permute-start.1 = (f32[104,128]{1,0:T(8,128)S(1)}, f32[104,128]{1,0:T(8,128)S(1)}, u32[]{:S(2)}, u32[]{:S(2)}) collective-permute-start(f32[104,128]{1,0:T(8,128)S(1)} %add.15), channel_id=1, source_target_pairs={{0,12},{1,13},{2,14},{3,15},{4,8},{5,9},{6,10},{7,11},{8,4},{9,5},... | collective-permute-start | bytes 159752 | tf_op jit(solution)/shard_map/ppermute | solution.py:341
  7.4 2.3 %collective-permute-done.1 = f32[104,128]{1,0:T(8,128)S(1)} collective-permute-done((f32[104,128]{1,0:T(8,128)S(1)}, f32[104,128]{1,0:T(8,128)S(1)}, u32[]{:S(2)}, u32[]{:S(2)}) %collective-permute-start.1) | collective-permute-done | bytes 53280 | tf_op jit(solution)/shard_map/ppermute | solution.py:341
  9.7 1.5 %collective-permute-start.2 = (f32[104,128]{1,0:T(8,128)S(1)}, f32[104,128]{1,0:T(8,128)S(1)}, u32[]{:S(2)}, u32[]{:S(2)}) collective-permute-start(f32[104,128]{1,0:T(8,128)S(1)} %add.16), channel_id=1, source_target_pairs={{0,20},{1,21},{2,22},{3,23},{4,16},{5,17},{6,18},{7,19},{8,28},{9,... | collective-permute-start | bytes 159752 | tf_op jit(solution)/shard_map/ppermute | solution.py:341
  11.3 2.3 %collective-permute-done.2 = f32[104,128]{1,0:T(8,128)S(1)} collective-permute-done((f32[104,128]{1,0:T(8,128)S(1)}, f32[104,128]{1,0:T(8,128)S(1)}, u32[]{:S(2)}, u32[]{:S(2)}) %collective-permute-start.2) | collective-permute-done | bytes 53280 | tf_op jit(solution)/shard_map/ppermute | solution.py:341
  13.6 0.5 %collective-permute-start.3 = (f32[104,128]{1,0:T(8,128)S(1)}, f32[104,128]{1,0:T(8,128)S(1)}, u32[]{:S(2)}, u32[]{:S(2)}) collective-permute-start(f32[104,128]{1,0:T(8,128)S(1)} %add.17), channel_id=1, source_target_pairs={{0,5},{1,4},{2,7},{3,6},{4,1},{5,0},{6,3},{7,2},{8,13},{9,12},{10,... | collective-permute-start | bytes 159752 | tf_op jit(solution)/shard_map/ppermute | solution.py:341
  14.1 3.4 %collective-permute-done.3 = f32[104,128]{1,0:T(8,128)S(1)} collective-permute-done((f32[104,128]{1,0:T(8,128)S(1)}, f32[104,128]{1,0:T(8,128)S(1)}, u32[]{:S(2)}, u32[]{:S(2)}) %collective-permute-start.3) | collective-permute-done | bytes 53280 | tf_op jit(solution)/shard_map/ppermute | solution.py:341
  17.5 0.4 %collective-permute-start.4 = (f32[104,128]{1,0:T(8,128)S(1)}, f32[104,128]{1,0:T(8,128)S(1)}, u32[]{:S(2)}, u32[]{:S(2)}) collective-permute-start(f32[104,128]{1,0:T(8,128)S(1)} %add.18), channel_id=1, source_target_pairs={{0,6},{1,7},{2,4},{3,5},{4,2},{5,3},{6,0},{7,1},{8,14},{9,15},{10,... | collective-permute-start | bytes 159752 | tf_op jit(solution)/shard_map/ppermute | solution.py:341
  17.9 5.7 %collective-permute-done.4 = f32[104,128]{1,0:T(8,128)S(1)} collective-permute-done((f32[104,128]{1,0:T(8,128)S(1)}, f32[104,128]{1,0:T(8,128)S(1)}, u32[]{:S(2)}, u32[]{:S(2)}) %collective-permute-start.4) | collective-permute-done | bytes 53280 | tf_op jit(solution)/shard_map/ppermute | solution.py:341
  23.6 0.5 %collective-permute-start.5 = (f32[104,128]{1,0:T(8,128)S(1)}, f32[104,128]{1,0:T(8,128)S(1)}, u32[]{:S(2)}, u32[]{:S(2)}) collective-permute-start(f32[104,128]{1,0:T(8,128)S(1)} %add.19.refs_0_), channel_id=1, source_target_pairs={{0,4},{1,5},{2,6},{3,7},{4,0},{5,1},{6,2},{7,3},{8,12},{9,13},{10,... | collective-permute-start | bytes 159752 | tf_op jit(solution)/shard_map/ppermute | solution.py:341
  24.1 0.9 %collective-permute-done.5.refs_1_ = f32[104,128]{1,0:T(8,128)S(1)} collective-permute-done((f32[104,128]{1,0:T(8,128)S(1)}, f32[104,128]{1,0:T(8,128)S(1)}, u32[]{:S(2)}, u32[]{:S(2)}) %collective-permute-start.5) | collective-permute-done | bytes 53280 | tf_op jit(solution)/shard_map/ppermute | solution.py:341
  25.0 5.1 %solve.1 = (f32[512]{0:T(512)}, f32[1024]{0:T(1024)}, f32[128,128]{1,0:T(8,128)}) custom-call(f32[104,128]{1,0:T(8,128)S(1)} %add.19.refs_0_, f32[104,128]{1,0:T(8,128)S(1)} %collective-permute-done.5.refs_1_), custom_call_target="tpu_custom_call" | custom-call | tf_op jit(solution)/shard_map/solve/pallas_call | solution.py:376
  (4 shorter events, 0.0 us)
Async XLA Ops:
  3.3 1.8 %collective-permute-start = (f32[104,128]{1,0:T(8,128)}, f32[104,128]{1,0:T(8,128)S(1)}, u32[]{:S(2)}, u32[]{:S(2)}) collective-permute-start(f32[104,128]{1,0:T(8,128)} %get-tuple-element.6), channel_id=1, source_target_pairs={{0,4},{1,5},{2,6},{3,7},{4,0},{5,1},{6,2},{7,3},{8,12},{9,13},{10,... | collective-permute-start | bytes 159752 | tf_op jit(solution)/shard_map/ppermute | solution.py:341
  5.9 3.8 %collective-permute-start.1 = (f32[104,128]{1,0:T(8,128)S(1)}, f32[104,128]{1,0:T(8,128)S(1)}, u32[]{:S(2)}, u32[]{:S(2)}) collective-permute-start(f32[104,128]{1,0:T(8,128)S(1)} %add.15), channel_id=1, source_target_pairs={{0,12},{1,13},{2,14},{3,15},{4,8},{5,9},{6,10},{7,11},{8,4},{9,5},... | collective-permute-start | bytes 159752 | tf_op jit(solution)/shard_map/ppermute | solution.py:341
  9.7 3.9 %collective-permute-start.2 = (f32[104,128]{1,0:T(8,128)S(1)}, f32[104,128]{1,0:T(8,128)S(1)}, u32[]{:S(2)}, u32[]{:S(2)}) collective-permute-start(f32[104,128]{1,0:T(8,128)S(1)} %add.16), channel_id=1, source_target_pairs={{0,20},{1,21},{2,22},{3,23},{4,16},{5,17},{6,18},{7,19},{8,28},{9,... | collective-permute-start | bytes 159752 | tf_op jit(solution)/shard_map/ppermute | solution.py:341
  13.6 3.9 %collective-permute-start.3 = (f32[104,128]{1,0:T(8,128)S(1)}, f32[104,128]{1,0:T(8,128)S(1)}, u32[]{:S(2)}, u32[]{:S(2)}) collective-permute-start(f32[104,128]{1,0:T(8,128)S(1)} %add.17), channel_id=1, source_target_pairs={{0,5},{1,4},{2,7},{3,6},{4,1},{5,0},{6,3},{7,2},{8,13},{9,12},{10,... | collective-permute-start | bytes 159752 | tf_op jit(solution)/shard_map/ppermute | solution.py:341
  17.5 6.1 %collective-permute-start.4 = (f32[104,128]{1,0:T(8,128)S(1)}, f32[104,128]{1,0:T(8,128)S(1)}, u32[]{:S(2)}, u32[]{:S(2)}) collective-permute-start(f32[104,128]{1,0:T(8,128)S(1)} %add.18), channel_id=1, source_target_pairs={{0,6},{1,7},{2,4},{3,5},{4,2},{5,3},{6,0},{7,1},{8,14},{9,15},{10,... | collective-permute-start | bytes 159752 | tf_op jit(solution)/shard_map/ppermute | solution.py:341
  23.6 1.3 %collective-permute-start.5 = (f32[104,128]{1,0:T(8,128)S(1)}, f32[104,128]{1,0:T(8,128)S(1)}, u32[]{:S(2)}, u32[]{:S(2)}) collective-permute-start(f32[104,128]{1,0:T(8,128)S(1)} %add.19.refs_0_), channel_id=1, source_target_pairs={{0,4},{1,5},{2,6},{3,7},{4,0},{5,1},{6,2},{7,3},{8,12},{9,13},{10,... | collective-permute-start | bytes 159752 | tf_op jit(solution)/shard_map/ppermute | solution.py:341
where the time goes:
time: 30.3 us; the launch traced here: 30.1 us
  waiting for transfers between devices  15.7 us (52%)
  Pallas kernels  7.77 us (26%)
  starting transfers between devices  5.06 us (17%)
  other arithmetic  0.85 us (3%)
  between operations  0.65 us (2%)
    ppermute x6, waiting for transfers between devices, swap(): return lax.ppermute(x, ('exp', 'imp'), pairs)  15.7 us
    pallas_call x1, Pallas kernels, per_device(): pl.pallas_call(functools.partial(solve_kernel, lay), out_shape=(jax.Shape...  5.12 us
    ppermute x6, starting transfers between devices, swap(): return lax.ppermute(x, ('exp', 'imp'), pairs)  5.06 us
    pallas_call x1, Pallas kernels, per_device(): pl.pallas_call(functools.partial(local_kernel, lay, slots), out_shape=[ja...  2.65 us
    add x1, other arithmetic, per_device(): mine = parts[0] + swap(parts[1], n_exp, n_imp, 1, 0)  0.82 us
  transfers between devices with their start and end apart: 6, of which 6 were waited for; matrix products, arithmetic and copies ran while one was open for 0% of the time, Pallas kernels for 0%

commit v1 on v0

--- a/solution.py
+++ b/solution.py
@@ -14,7 +14,6 @@
 LANES = 128
 RIDGE = 64.0
 VMEM_BYTES = 48 * 1024 * 1024
-LOCAL_BYTES = 56 * 1024 * 1024
 
 f32 = jnp.float32
 bf16 = jnp.bfloat16
@@ -51,7 +50,7 @@
 
 
 def half_of(exp_place, imp_place):
-    bits = exp_place ^ imp_place
+    bits = exp_place ^ (imp_place & 1)
     for shift in (8, 4, 2, 1):
         bits = bits ^ (bits >> shift)
     return bits & 1
@@ -59,8 +58,11 @@
 
 def local_kernel(lay, slots, *refs):
     sources, outs, out, homes, sems = refs[:5], refs[5:7], refs[7], refs[8:13], refs[13]
-    copies = [pltpu.make_async_copy(x, y, sems.at[j]) for j, (x, y) in enumerate(zip(sources, homes))]
-    for copy in copies:
+    small = [pltpu.make_async_copy(sources[j], homes[j], sems.at[j]) for j in range(1, 5)]
+    tiles = [
+        pltpu.make_async_copy(sources[0].at[k], homes[0].at[k], sems.at[5 + k]) for k in range(slots)
+    ]
+    for copy in small + tiles:
         copy.start()
     flows, routing, tile_block, ec, ic = homes
     exp_place, imp_place = lax.axis_index("exp"), lax.axis_index("imp")
@@ -71,8 +73,18 @@
     per = side // LANES
     country = iota((NCE, side), 0)
     ones = jnp.ones((8, side), bf16)
-    for copy in copies:
+    for copy in small:
         copy.wait()
+    cnt_a = jnp.zeros((8, LANES), f32)
+    for r in range(row_blocks):
+        cnt_a += dot(ones, (country == ec[r]).astype(f32).astype(bf16), 1, 1)
+    cnt_b = jnp.zeros((8, LANES), f32)
+    for c in range(col_local):
+        cnt_b += dot(ones, (country == ic[c]).astype(f32).astype(bf16), 1, 1)
+    cnt_a = cnt_a[0:1] * (imp_place == 0).astype(f32)
+    cnt_b = cnt_b[0:1] * (exp_place == 0).astype(f32)
+    out[lay.cnt_at : lay.cnt_at + 1, :] = cnt_a
+    out[lay.cnt_at + 1 : lay.cnt_at + 2, :] = cnt_b
     pairs = jnp.zeros((NCE, NCI), f32)
     for k in range(slots):
         r = tile_block[k] // col_local
@@ -83,12 +95,15 @@
         keep = live.astype(f32)
         hot_r = (country == ec[r]).astype(f32).astype(bf16)
         hot_c = (country == ic[c]).astype(f32).astype(bf16)
+        tiles[k].wait()
         tile = flows[k] * keep.astype(bf16)
         half = dot(hot_r, tile, 1, 0)
         col_sum = jnp.sum(half, axis=0, keepdims=True)
         row_sum = dot(ones, tile, 1, 1)[0:1]
-        for piece in split(half):
-            pairs = pairs + dot(piece.astype(bf16), hot_c, 1, 1)
+        top = half.astype(bf16)
+        rest = (half - top.astype(f32)).astype(bf16)
+        both = dot(jnp.concatenate([top, rest], axis=0), hot_c, 1, 1)
+        pairs = pairs + (both[:NCE] + both[NCE:])
         row_at = lay.rows_at + (exp_place * row_blocks + r) * per
         col_at = lay.cols_at + (imp_place * col_local + c) * per
         for h in range(per):
@@ -99,16 +114,6 @@
         here = iota((1, LANES), 1) == flat % LANES
         out[pl.ds(lay.live_at + flat // LANES, 1), :] += jnp.where(here, keep, 0.0)
     out[0:NCE, :] = pairs
-    cnt_a = jnp.zeros((8, LANES), f32)
-    for r in range(row_blocks):
-        cnt_a += dot(ones, (country == ec[r]).astype(f32).astype(bf16), 1, 1)
-    cnt_b = jnp.zeros((8, LANES), f32)
-    for c in range(col_local):
-        cnt_b += dot(ones, (country == ic[c]).astype(f32).astype(bf16), 1, 1)
-    cnt_a = cnt_a[0:1] * (imp_place == 0).astype(f32)
-    cnt_b = cnt_b[0:1] * (exp_place == 0).astype(f32)
-    out[lay.cnt_at : lay.cnt_at + 1, :] = cnt_a
-    out[lay.cnt_at + 1 : lay.cnt_at + 2, :] = cnt_b
     mine = half_of(exp_place, imp_place)
     for k, part in enumerate(outs):
         part[...] = out[pl.ds(pl.multiple_of((mine ^ k) * lay.share, 8), lay.share), :]
@@ -354,6 +359,7 @@
         exp_country.reshape(-1, 1, side),
         imp_country.reshape(-1, 1, side),
     )
+    inputs = tuple(pltpu.with_memory_space_constraint(x, pltpu.HBM) for x in inputs)
     homes = [pltpu.VMEM, pltpu.SMEM, pltpu.SMEM, pltpu.VMEM, pltpu.VMEM]
     parts = pl.pallas_call(
         functools.partial(local_kernel, lay, slots),
@@ -362,15 +368,15 @@
         out_specs=[vmem] * 2,
         scratch_shapes=[pltpu.VMEM((2 * lay.share, LANES), f32)]
         + [space(x.shape, x.dtype) for space, x in zip(homes, inputs)]
-        + [pltpu.SemaphoreType.DMA((5,))],
-        compiler_params=pltpu.CompilerParams(vmem_limit_bytes=LOCAL_BYTES),
+        + [pltpu.SemaphoreType.DMA((5 + slots,))],
+        compiler_params=pltpu.CompilerParams(vmem_limit_bytes=VMEM_BYTES),
         name="local_sums",
     )(*inputs)
     mine = parts[0] + swap(parts[1], n_exp, n_imp, 1, 0)
     for bit in powers(2, n_exp):
         mine = mine + swap(mine, n_exp, n_imp, bit | 1, 0)
     for bit in powers(1, n_imp):
-        mine = mine + swap(mine, n_exp, n_imp, 1, bit)
+        mine = mine + swap(mine, n_exp, n_imp, 1, 2 * bit - 1)
     shares = (mine, swap(mine, n_exp, n_imp, 1, 0))
     high = 16
     a, b, g = pl.pallas_call(

time: 30.3 us -> 29.3 us (0.967)
  the two profiles are of different devices: /device:TPU:25 before, /device:TPU:0 now
where the time goes in v1:
time: 29.3 us; the launch traced here: 29.1 us
  starting transfers between devices  11.6 us (40%)
  waiting for transfers between devices  9.57 us (33%)
  Pallas kernels  7.3 us (25%)
  between operations  0.65 us (2%)
    ppermute x6, starting transfers between devices, swap(): return lax.ppermute(x, ('exp', 'imp'), pairs)  11.6 us
    ppermute x6, waiting for transfers between devices, swap(): return lax.ppermute(x, ('exp', 'imp'), pairs)  9.57 us
    pallas_call x1, Pallas kernels, per_device(): pl.pallas_call(functools.partial(solve_kernel, lay), out_shape=(jax.Shape...  5.12 us
    pallas_call x1, Pallas kernels, per_device(): pl.pallas_call(functools.partial(local_kernel, lay, slots), out_shape=[ja...  2.18 us
  transfers between devices with their start and end apart: 6, of which 6 were waited for; matrix products, arithmetic and copies ran while one was open for 0% of the time, Pallas kernels for 0%

profile of v1, /device:TPU:0, one launch (start us, length us, event | category | flops | bytes accessed | tf_op | source)
XLA Modules:
  0.0 29.1 jit_solution(5232625340049891287)
XLA Ops:
  0.6 2.2 %local_sums.1 = (f32[104,128]{1,0:T(8,128)S(1)}, f32[104,128]{1,0:T(8,128)S(1)}) custom-call(bf16[4,256,256]{2,1,0:T(8,128)(2,1)} %refs_0_.1, s32[4]{0:T(128)} %bitcast.5, s32[4]{0:T(128)} %refs_2_.1, s32[2,1,256]{2,1,0:T(1,128)} %bitcast.4, s32[4,1,256]{2,1,0:T(1,128)} %bitcast.3), custom_call_target="tpu_custom_call" | custom-call | tf_op jit(solution)/shard_map/local_sums/pallas_call | solution.py:364
  2.8 0.5 %collective-permute-start = (f32[104,128]{1,0:T(8,128)S(1)}, f32[104,128]{1,0:T(8,128)S(1)}, u32[]{:S(2)}, u32[]{:S(2)}) collective-permute-start(f32[104,128]{1,0:T(8,128)S(1)} %get-tuple-element.6), channel_id=1, source_target_pairs={{0,4},{1,5},{2,6},{3,7},{4,0},{5,1},{6,2},{7,3},{8,12},{9,13},{10,... | collective-permute-start | bytes 159752 | tf_op jit(solution)/shard_map/ppermute | solution.py:346
  3.3 0.9 %collective-permute-done = f32[104,128]{1,0:T(8,128)S(1)} collective-permute-done((f32[104,128]{1,0:T(8,128)S(1)}, f32[104,128]{1,0:T(8,128)S(1)}, u32[]{:S(2)}, u32[]{:S(2)}) %collective-permute-start) | collective-permute-done | bytes 53280 | tf_op jit(solution)/shard_map/ppermute | solution.py:346
  4.2 2.6 %collective-permute-start.1 = (f32[104,128]{1,0:T(8,128)S(1)}, f32[104,128]{1,0:T(8,128)S(1)}, u32[]{:S(2)}, u32[]{:S(2)}) collective-permute-start(f32[104,128]{1,0:T(8,128)S(1)} %add.15), channel_id=1, source_target_pairs={{0,12},{1,13},{2,14},{3,15},{4,8},{5,9},{6,10},{7,11},{8,4},{9,5},... | collective-permute-start | bytes 159752 | tf_op jit(solution)/shard_map/ppermute | solution.py:346
  6.8 1.9 %collective-permute-done.1 = f32[104,128]{1,0:T(8,128)S(1)} collective-permute-done((f32[104,128]{1,0:T(8,128)S(1)}, f32[104,128]{1,0:T(8,128)S(1)}, u32[]{:S(2)}, u32[]{:S(2)}) %collective-permute-start.1) | collective-permute-done | bytes 53280 | tf_op jit(solution)/shard_map/ppermute | solution.py:346
  8.8 2.0 %collective-permute-start.2 = (f32[104,128]{1,0:T(8,128)S(1)}, f32[104,128]{1,0:T(8,128)S(1)}, u32[]{:S(2)}, u32[]{:S(2)}) collective-permute-start(f32[104,128]{1,0:T(8,128)S(1)} %add.16), channel_id=1, source_target_pairs={{0,20},{1,21},{2,22},{3,23},{4,16},{5,17},{6,18},{7,19},{8,28},{9,... | collective-permute-start | bytes 159752 | tf_op jit(solution)/shard_map/ppermute | solution.py:346
  10.8 1.9 %collective-permute-done.2 = f32[104,128]{1,0:T(8,128)S(1)} collective-permute-done((f32[104,128]{1,0:T(8,128)S(1)}, f32[104,128]{1,0:T(8,128)S(1)}, u32[]{:S(2)}, u32[]{:S(2)}) %collective-permute-start.2) | collective-permute-done | bytes 53280 | tf_op jit(solution)/shard_map/ppermute | solution.py:346
  12.7 2.0 %collective-permute-start.3 = (f32[104,128]{1,0:T(8,128)S(1)}, f32[104,128]{1,0:T(8,128)S(1)}, u32[]{:S(2)}, u32[]{:S(2)}) collective-permute-start(f32[104,128]{1,0:T(8,128)S(1)} %add.17), channel_id=1, source_target_pairs={{0,5},{1,4},{2,7},{3,6},{4,1},{5,0},{6,3},{7,2},{8,13},{9,12},{10,... | collective-permute-start | bytes 159752 | tf_op jit(solution)/shard_map/ppermute | solution.py:346
  14.8 1.9 %collective-permute-done.3 = f32[104,128]{1,0:T(8,128)S(1)} collective-permute-done((f32[104,128]{1,0:T(8,128)S(1)}, f32[104,128]{1,0:T(8,128)S(1)}, u32[]{:S(2)}, u32[]{:S(2)}) %collective-permute-start.3) | collective-permute-done | bytes 53280 | tf_op jit(solution)/shard_map/ppermute | solution.py:346
  16.7 4.0 %collective-permute-start.4 = (f32[104,128]{1,0:T(8,128)S(1)}, f32[104,128]{1,0:T(8,128)S(1)}, u32[]{:S(2)}, u32[]{:S(2)}) collective-permute-start(f32[104,128]{1,0:T(8,128)S(1)} %add.18), channel_id=1, source_target_pairs={{0,7},{1,6},{2,5},{3,4},{4,3},{5,2},{6,1},{7,0},{8,15},{9,14},{10,... | collective-permute-start | bytes 159752 | tf_op jit(solution)/shard_map/ppermute | solution.py:346
  20.7 2.0 %collective-permute-done.4 = f32[104,128]{1,0:T(8,128)S(1)} collective-permute-done((f32[104,128]{1,0:T(8,128)S(1)}, f32[104,128]{1,0:T(8,128)S(1)}, u32[]{:S(2)}, u32[]{:S(2)}) %collective-permute-start.4) | collective-permute-done | bytes 53280 | tf_op jit(solution)/shard_map/ppermute | solution.py:346
  22.7 0.4 %collective-permute-start.5 = (f32[104,128]{1,0:T(8,128)S(1)}, f32[104,128]{1,0:T(8,128)S(1)}, u32[]{:S(2)}, u32[]{:S(2)}) collective-permute-start(f32[104,128]{1,0:T(8,128)S(1)} %add.19.refs_0_), channel_id=1, source_target_pairs={{0,4},{1,5},{2,6},{3,7},{4,0},{5,1},{6,2},{7,3},{8,12},{9,13},{10,... | collective-permute-start | bytes 159752 | tf_op jit(solution)/shard_map/ppermute | solution.py:346
  23.1 0.9 %collective-permute-done.5.refs_1_ = f32[104,128]{1,0:T(8,128)S(1)} collective-permute-done((f32[104,128]{1,0:T(8,128)S(1)}, f32[104,128]{1,0:T(8,128)S(1)}, u32[]{:S(2)}, u32[]{:S(2)}) %collective-permute-start.5) | collective-permute-done | bytes 53280 | tf_op jit(solution)/shard_map/ppermute | solution.py:346
  24.0 5.1 %solve.1 = (f32[512]{0:T(512)}, f32[1024]{0:T(1024)}, f32[128,128]{1,0:T(8,128)}) custom-call(f32[104,128]{1,0:T(8,128)S(1)} %add.19.refs_0_, f32[104,128]{1,0:T(8,128)S(1)} %collective-permute-done.5.refs_1_), custom_call_target="tpu_custom_call" | custom-call | tf_op jit(solution)/shard_map/solve/pallas_call | solution.py:382
  (5 shorter events, 0.0 us)
Async XLA Ops:
  2.8 1.4 %collective-permute-start = (f32[104,128]{1,0:T(8,128)S(1)}, f32[104,128]{1,0:T(8,128)S(1)}, u32[]{:S(2)}, u32[]{:S(2)}) collective-permute-start(f32[104,128]{1,0:T(8,128)S(1)} %get-tuple-element.6), channel_id=1, source_target_pairs={{0,4},{1,5},{2,6},{3,7},{4,0},{5,1},{6,2},{7,3},{8,12},{9,13},{10,... | collective-permute-start | bytes 159752 | tf_op jit(solution)/shard_map/ppermute | solution.py:346
  4.2 4.6 %collective-permute-start.1 = (f32[104,128]{1,0:T(8,128)S(1)}, f32[104,128]{1,0:T(8,128)S(1)}, u32[]{:S(2)}, u32[]{:S(2)}) collective-permute-start(f32[104,128]{1,0:T(8,128)S(1)} %add.15), channel_id=1, source_target_pairs={{0,12},{1,13},{2,14},{3,15},{4,8},{5,9},{6,10},{7,11},{8,4},{9,5},... | collective-permute-start | bytes 159752 | tf_op jit(solution)/shard_map/ppermute | solution.py:346
  8.8 3.9 %collective-permute-start.2 = (f32[104,128]{1,0:T(8,128)S(1)}, f32[104,128]{1,0:T(8,128)S(1)}, u32[]{:S(2)}, u32[]{:S(2)}) collective-permute-start(f32[104,128]{1,0:T(8,128)S(1)} %add.16), channel_id=1, source_target_pairs={{0,20},{1,21},{2,22},{3,23},{4,16},{5,17},{6,18},{7,19},{8,28},{9,... | collective-permute-start | bytes 159752 | tf_op jit(solution)/shard_map/ppermute | solution.py:346
  12.7 4.0 %collective-permute-start.3 = (f32[104,128]{1,0:T(8,128)S(1)}, f32[104,128]{1,0:T(8,128)S(1)}, u32[]{:S(2)}, u32[]{:S(2)}) collective-permute-start(f32[104,128]{1,0:T(8,128)S(1)} %add.17), channel_id=1, source_target_pairs={{0,5},{1,4},{2,7},{3,6},{4,1},{5,0},{6,3},{7,2},{8,13},{9,12},{10,... | collective-permute-start | bytes 159752 | tf_op jit(solution)/shard_map/ppermute | solution.py:346
  16.7 6.0 %collective-permute-start.4 = (f32[104,128]{1,0:T(8,128)S(1)}, f32[104,128]{1,0:T(8,128)S(1)}, u32[]{:S(2)}, u32[]{:S(2)}) collective-permute-start(f32[104,128]{1,0:T(8,128)S(1)} %add.18), channel_id=1, source_target_pairs={{0,7},{1,6},{2,5},{3,4},{4,3},{5,2},{6,1},{7,0},{8,15},{9,14},{10,... | collective-permute-start | bytes 159752 | tf_op jit(solution)/shard_map/ppermute | solution.py:346
  22.7 1.3 %collective-permute-start.5 = (f32[104,128]{1,0:T(8,128)S(1)}, f32[104,128]{1,0:T(8,128)S(1)}, u32[]{:S(2)}, u32[]{:S(2)}) collective-permute-start(f32[104,128]{1,0:T(8,128)S(1)} %add.19.refs_0_), channel_id=1, source_target_pairs={{0,4},{1,5},{2,6},{3,7},{4,0},{5,1},{6,2},{7,3},{8,12},{9,13},{10,... | collective-permute-start | bytes 159752 | tf_op jit(solution)/shard_map/ppermute | solution.py:346

commit v2 on v1

--- a/solution.py
+++ b/solution.py
@@ -160,10 +160,12 @@
             jump //= 2
         self.country = country
         self.second = place >= lookup(middle, country)
+        at = iota((block, LANES), 0).astype(f32).astype(bf16)
+        one, none = jnp.ones((block, LANES), bf16), jnp.zeros((block, LANES), bf16)
         for j in range(n // block):
-            at = (iota((block, LANES), 0) + j * block).astype(f32)
-            inside = (at >= start) & (at < end)
-            hot[j * block : (j + 1) * block, :] = jnp.where(inside, 1.0, 0.0).astype(bf16)
+            lo, hi = (jnp.clip(x - j * block, 0.0, block).astype(bf16) for x in (start, end))
+            inside = (at >= lo) & (at < hi)
+            hot[j * block : (j + 1) * block, :] = jnp.where(inside, one, none)
 
     def expand(self, first, second):
         return jnp.where(self.second, lookup(second, self.country), lookup(first, self.country))

time: 29.3 us -> 29.1 us (level)
  no operation moved by 1% of the time
where the time goes in v2:
time: 29.1 us; the launch traced here: 29 us
  starting transfers between devices  11.6 us (40%)
  waiting for transfers between devices  9.57 us (33%)
  Pallas kernels  7.16 us (25%)
  between operations  0.65 us (2%)
    ppermute x6, starting transfers between devices, swap(): return lax.ppermute(x, ('exp', 'imp'), pairs)  11.6 us
    ppermute x6, waiting for transfers between devices, swap(): return lax.ppermute(x, ('exp', 'imp'), pairs)  9.57 us
    pallas_call x1, Pallas kernels, per_device(): pl.pallas_call(functools.partial(solve_kernel, lay), out_shape=(jax.Shape...  4.98 us
    pallas_call x1, Pallas kernels, per_device(): pl.pallas_call(functools.partial(local_kernel, lay, slots), out_shape=[ja...  2.18 us
  transfers between devices with their start and end apart: 6, of which 6 were waited for; matrix products, arithmetic and copies ran while one was open for 0% of the time, Pallas kernels for 0%

profile of v2, /device:TPU:0, one launch (start us, length us, event | category | flops | bytes accessed | tf_op | source)
XLA Modules:
  0.0 29.0 jit_solution(972095568314168120)
XLA Ops:
  0.6 2.2 %local_sums.1 = (f32[104,128]{1,0:T(8,128)S(1)}, f32[104,128]{1,0:T(8,128)S(1)}) custom-call(bf16[4,256,256]{2,1,0:T(8,128)(2,1)} %refs_0_.1, s32[4]{0:T(128)} %bitcast.5, s32[4]{0:T(128)} %refs_2_.1, s32[2,1,256]{2,1,0:T(1,128)} %bitcast.4, s32[4,1,256]{2,1,0:T(1,128)} %bitcast.3), custom_call_target="tpu_custom_call" | custom-call | tf_op jit(solution)/shard_map/local_sums/pallas_call | solution.py:366
  2.8 0.5 %collective-permute-start = (f32[104,128]{1,0:T(8,128)S(1)}, f32[104,128]{1,0:T(8,128)S(1)}, u32[]{:S(2)}, u32[]{:S(2)}) collective-permute-start(f32[104,128]{1,0:T(8,128)S(1)} %get-tuple-element.6), channel_id=1, source_target_pairs={{0,4},{1,5},{2,6},{3,7},{4,0},{5,1},{6,2},{7,3},{8,12},{9,13},{10,... | collective-permute-start | bytes 159752 | tf_op jit(solution)/shard_map/ppermute | solution.py:348
  3.3 0.9 %collective-permute-done = f32[104,128]{1,0:T(8,128)S(1)} collective-permute-done((f32[104,128]{1,0:T(8,128)S(1)}, f32[104,128]{1,0:T(8,128)S(1)}, u32[]{:S(2)}, u32[]{:S(2)}) %collective-permute-start) | collective-permute-done | bytes 53280 | tf_op jit(solution)/shard_map/ppermute | solution.py:348
  4.2 2.6 %collective-permute-start.1 = (f32[104,128]{1,0:T(8,128)S(1)}, f32[104,128]{1,0:T(8,128)S(1)}, u32[]{:S(2)}, u32[]{:S(2)}) collective-permute-start(f32[104,128]{1,0:T(8,128)S(1)} %add.15), channel_id=1, source_target_pairs={{0,12},{1,13},{2,14},{3,15},{4,8},{5,9},{6,10},{7,11},{8,4},{9,5},... | collective-permute-start | bytes 159752 | tf_op jit(solution)/shard_map/ppermute | solution.py:348
  6.8 1.9 %collective-permute-done.1 = f32[104,128]{1,0:T(8,128)S(1)} collective-permute-done((f32[104,128]{1,0:T(8,128)S(1)}, f32[104,128]{1,0:T(8,128)S(1)}, u32[]{:S(2)}, u32[]{:S(2)}) %collective-permute-start.1) | collective-permute-done | bytes 53280 | tf_op jit(solution)/shard_map/ppermute | solution.py:348
  8.8 2.0 %collective-permute-start.2 = (f32[104,128]{1,0:T(8,128)S(1)}, f32[104,128]{1,0:T(8,128)S(1)}, u32[]{:S(2)}, u32[]{:S(2)}) collective-permute-start(f32[104,128]{1,0:T(8,128)S(1)} %add.16), channel_id=1, source_target_pairs={{0,20},{1,21},{2,22},{3,23},{4,16},{5,17},{6,18},{7,19},{8,28},{9,... | collective-permute-start | bytes 159752 | tf_op jit(solution)/shard_map/ppermute | solution.py:348
  10.8 1.9 %collective-permute-done.2 = f32[104,128]{1,0:T(8,128)S(1)} collective-permute-done((f32[104,128]{1,0:T(8,128)S(1)}, f32[104,128]{1,0:T(8,128)S(1)}, u32[]{:S(2)}, u32[]{:S(2)}) %collective-permute-start.2) | collective-permute-done | bytes 53280 | tf_op jit(solution)/shard_map/ppermute | solution.py:348
  12.7 2.0 %collective-permute-start.3 = (f32[104,128]{1,0:T(8,128)S(1)}, f32[104,128]{1,0:T(8,128)S(1)}, u32[]{:S(2)}, u32[]{:S(2)}) collective-permute-start(f32[104,128]{1,0:T(8,128)S(1)} %add.17), channel_id=1, source_target_pairs={{0,5},{1,4},{2,7},{3,6},{4,1},{5,0},{6,3},{7,2},{8,13},{9,12},{10,... | collective-permute-start | bytes 159752 | tf_op jit(solution)/shard_map/ppermute | solution.py:348
  14.8 1.9 %collective-permute-done.3 = f32[104,128]{1,0:T(8,128)S(1)} collective-permute-done((f32[104,128]{1,0:T(8,128)S(1)}, f32[104,128]{1,0:T(8,128)S(1)}, u32[]{:S(2)}, u32[]{:S(2)}) %collective-permute-start.3) | collective-permute-done | bytes 53280 | tf_op jit(solution)/shard_map/ppermute | solution.py:348
  16.7 4.0 %collective-permute-start.4 = (f32[104,128]{1,0:T(8,128)S(1)}, f32[104,128]{1,0:T(8,128)S(1)}, u32[]{:S(2)}, u32[]{:S(2)}) collective-permute-start(f32[104,128]{1,0:T(8,128)S(1)} %add.18), channel_id=1, source_target_pairs={{0,7},{1,6},{2,5},{3,4},{4,3},{5,2},{6,1},{7,0},{8,15},{9,14},{10,... | collective-permute-start | bytes 159752 | tf_op jit(solution)/shard_map/ppermute | solution.py:348
  20.7 2.0 %collective-permute-done.4 = f32[104,128]{1,0:T(8,128)S(1)} collective-permute-done((f32[104,128]{1,0:T(8,128)S(1)}, f32[104,128]{1,0:T(8,128)S(1)}, u32[]{:S(2)}, u32[]{:S(2)}) %collective-permute-start.4) | collective-permute-done | bytes 53280 | tf_op jit(solution)/shard_map/ppermute | solution.py:348
  22.7 0.4 %collective-permute-start.5 = (f32[104,128]{1,0:T(8,128)S(1)}, f32[104,128]{1,0:T(8,128)S(1)}, u32[]{:S(2)}, u32[]{:S(2)}) collective-permute-start(f32[104,128]{1,0:T(8,128)S(1)} %add.19.refs_0_), channel_id=1, source_target_pairs={{0,4},{1,5},{2,6},{3,7},{4,0},{5,1},{6,2},{7,3},{8,12},{9,13},{10,... | collective-permute-start | bytes 159752 | tf_op jit(solution)/shard_map/ppermute | solution.py:348
  23.1 0.9 %collective-permute-done.5.refs_1_ = f32[104,128]{1,0:T(8,128)S(1)} collective-permute-done((f32[104,128]{1,0:T(8,128)S(1)}, f32[104,128]{1,0:T(8,128)S(1)}, u32[]{:S(2)}, u32[]{:S(2)}) %collective-permute-start.5) | collective-permute-done | bytes 53280 | tf_op jit(solution)/shard_map/ppermute | solution.py:348
  24.0 5.0 %solve.1 = (f32[512]{0:T(512)}, f32[1024]{0:T(1024)}, f32[128,128]{1,0:T(8,128)}) custom-call(f32[104,128]{1,0:T(8,128)S(1)} %add.19.refs_0_, f32[104,128]{1,0:T(8,128)S(1)} %collective-permute-done.5.refs_1_), custom_call_target="tpu_custom_call" | custom-call | tf_op jit(solution)/shard_map/solve/pallas_call | solution.py:384
  (5 shorter events, 0.0 us)
Async XLA Ops:
  2.8 1.4 %collective-permute-start = (f32[104,128]{1,0:T(8,128)S(1)}, f32[104,128]{1,0:T(8,128)S(1)}, u32[]{:S(2)}, u32[]{:S(2)}) collective-permute-start(f32[104,128]{1,0:T(8,128)S(1)} %get-tuple-element.6), channel_id=1, source_target_pairs={{0,4},{1,5},{2,6},{3,7},{4,0},{5,1},{6,2},{7,3},{8,12},{9,13},{10,... | collective-permute-start | bytes 159752 | tf_op jit(solution)/shard_map/ppermute | solution.py:348
  4.2 4.6 %collective-permute-start.1 = (f32[104,128]{1,0:T(8,128)S(1)}, f32[104,128]{1,0:T(8,128)S(1)}, u32[]{:S(2)}, u32[]{:S(2)}) collective-permute-start(f32[104,128]{1,0:T(8,128)S(1)} %add.15), channel_id=1, source_target_pairs={{0,12},{1,13},{2,14},{3,15},{4,8},{5,9},{6,10},{7,11},{8,4},{9,5},... | collective-permute-start | bytes 159752 | tf_op jit(solution)/shard_map/ppermute | solution.py:348
  8.8 3.9 %collective-permute-start.2 = (f32[104,128]{1,0:T(8,128)S(1)}, f32[104,128]{1,0:T(8,128)S(1)}, u32[]{:S(2)}, u32[]{:S(2)}) collective-permute-start(f32[104,128]{1,0:T(8,128)S(1)} %add.16), channel_id=1, source_target_pairs={{0,20},{1,21},{2,22},{3,23},{4,16},{5,17},{6,18},{7,19},{8,28},{9,... | collective-permute-start | bytes 159752 | tf_op jit(solution)/shard_map/ppermute | solution.py:348
  12.7 4.0 %collective-permute-start.3 = (f32[104,128]{1,0:T(8,128)S(1)}, f32[104,128]{1,0:T(8,128)S(1)}, u32[]{:S(2)}, u32[]{:S(2)}) collective-permute-start(f32[104,128]{1,0:T(8,128)S(1)} %add.17), channel_id=1, source_target_pairs={{0,5},{1,4},{2,7},{3,6},{4,1},{5,0},{6,3},{7,2},{8,13},{9,12},{10,... | collective-permute-start | bytes 159752 | tf_op jit(solution)/shard_map/ppermute | solution.py:348
  16.7 6.0 %collective-permute-start.4 = (f32[104,128]{1,0:T(8,128)S(1)}, f32[104,128]{1,0:T(8,128)S(1)}, u32[]{:S(2)}, u32[]{:S(2)}) collective-permute-start(f32[104,128]{1,0:T(8,128)S(1)} %add.18), channel_id=1, source_target_pairs={{0,7},{1,6},{2,5},{3,4},{4,3},{5,2},{6,1},{7,0},{8,15},{9,14},{10,... | collective-permute-start | bytes 159752 | tf_op jit(solution)/shard_map/ppermute | solution.py:348
  22.7 1.3 %collective-permute-start.5 = (f32[104,128]{1,0:T(8,128)S(1)}, f32[104,128]{1,0:T(8,128)S(1)}, u32[]{:S(2)}, u32[]{:S(2)}) collective-permute-start(f32[104,128]{1,0:T(8,128)S(1)} %add.19.refs_0_), channel_id=1, source_target_pairs={{0,4},{1,5},{2,6},{3,7},{4,0},{5,1},{6,2},{7,3},{8,12},{9,13},{10,... | collective-permute-start | bytes 159752 | tf_op jit(solution)/shard_map/ppermute | solution.py:348

commit v3 on v2

--- a/solution.py
+++ b/solution.py
@@ -50,7 +50,7 @@
 
 
 def half_of(exp_place, imp_place):
-    bits = exp_place ^ (imp_place & 1)
+    bits = exp_place ^ imp_place
     for shift in (8, 4, 2, 1):
         bits = bits ^ (bits >> shift)
     return bits & 1
@@ -378,7 +378,7 @@
     for bit in powers(2, n_exp):
         mine = mine + swap(mine, n_exp, n_imp, bit | 1, 0)
     for bit in powers(1, n_imp):
-        mine = mine + swap(mine, n_exp, n_imp, 1, 2 * bit - 1)
+        mine = mine + swap(mine, n_exp, n_imp, 1, bit)
     shares = (mine, swap(mine, n_exp, n_imp, 1, 0))
     high = 16
     a, b, g = pl.pallas_call(

time: 29.1 us -> 28.7 us (0.986)
  the two profiles are of different devices: /device:TPU:0 before, /device:TPU:29 now
where the time goes in v3:
time: 28.7 us; the launch traced here: 28.6 us
  waiting for transfers between devices  16.5 us (57%)
  Pallas kernels  7.16 us (25%)
  starting transfers between devices  4.19 us (15%)
  between operations  0.65 us (2%)
    ppermute x6, waiting for transfers between devices, swap(): return lax.ppermute(x, ('exp', 'imp'), pairs)  16.5 us
    pallas_call x1, Pallas kernels, per_device(): pl.pallas_call(functools.partial(solve_kernel, lay), out_shape=(jax.Shape...  4.98 us
    ppermute x6, starting transfers between devices, swap(): return lax.ppermute(x, ('exp', 'imp'), pairs)  4.19 us
    pallas_call x1, Pallas kernels, per_device(): pl.pallas_call(functools.partial(local_kernel, lay, slots), out_shape=[ja...  2.18 us
  transfers between devices with their start and end apart: 6, of which 6 were waited for; matrix products, arithmetic and copies ran while one was open for 0% of the time, Pallas kernels for 0%

profile of v3, /device:TPU:29, one launch (start us, length us, event | category | flops | bytes accessed | tf_op | source)
XLA Modules:
  0.0 28.6 jit_solution(5887238987570619867)
XLA Ops:
  0.6 2.2 %local_sums.1 = (f32[104,128]{1,0:T(8,128)S(1)}, f32[104,128]{1,0:T(8,128)S(1)}) custom-call(bf16[4,256,256]{2,1,0:T(8,128)(2,1)} %refs_0_.1, s32[4]{0:T(128)} %bitcast.5, s32[4]{0:T(128)} %refs_2_.1, s32[2,1,256]{2,1,0:T(1,128)} %bitcast.4, s32[4,1,256]{2,1,0:T(1,128)} %bitcast.3), custom_call_target="tpu_custom_call" | custom-call | tf_op jit(solution)/shard_map/local_sums/pallas_call | solution.py:366
  2.8 0.7 %collective-permute-start = (f32[104,128]{1,0:T(8,128)S(1)}, f32[104,128]{1,0:T(8,128)S(1)}, u32[]{:S(2)}, u32[]{:S(2)}) collective-permute-start(f32[104,128]{1,0:T(8,128)S(1)} %get-tuple-element.6), channel_id=1, source_target_pairs={{0,4},{1,5},{2,6},{3,7},{4,0},{5,1},{6,2},{7,3},{8,12},{9,13},{10,... | collective-permute-start | bytes 159752 | tf_op jit(solution)/shard_map/ppermute | solution.py:348
  3.6 0.9 %collective-permute-done = f32[104,128]{1,0:T(8,128)S(1)} collective-permute-done((f32[104,128]{1,0:T(8,128)S(1)}, f32[104,128]{1,0:T(8,128)S(1)}, u32[]{:S(2)}, u32[]{:S(2)}) %collective-permute-start) | collective-permute-done | bytes 53280 | tf_op jit(solution)/shard_map/ppermute | solution.py:348
  4.4 1.5 %collective-permute-start.1 = (f32[104,128]{1,0:T(8,128)S(1)}, f32[104,128]{1,0:T(8,128)S(1)}, u32[]{:S(2)}, u32[]{:S(2)}) collective-permute-start(f32[104,128]{1,0:T(8,128)S(1)} %add.15), channel_id=1, source_target_pairs={{0,12},{1,13},{2,14},{3,15},{4,8},{5,9},{6,10},{7,11},{8,4},{9,5},... | collective-permute-start | bytes 159752 | tf_op jit(solution)/shard_map/ppermute | solution.py:348
  6.0 2.3 %collective-permute-done.1 = f32[104,128]{1,0:T(8,128)S(1)} collective-permute-done((f32[104,128]{1,0:T(8,128)S(1)}, f32[104,128]{1,0:T(8,128)S(1)}, u32[]{:S(2)}, u32[]{:S(2)}) %collective-permute-start.1) | collective-permute-done | bytes 53280 | tf_op jit(solution)/shard_map/ppermute | solution.py:348
  8.3 0.6 %collective-permute-start.2 = (f32[104,128]{1,0:T(8,128)S(1)}, f32[104,128]{1,0:T(8,128)S(1)}, u32[]{:S(2)}, u32[]{:S(2)}) collective-permute-start(f32[104,128]{1,0:T(8,128)S(1)} %add.16), channel_id=1, source_target_pairs={{0,20},{1,21},{2,22},{3,23},{4,16},{5,17},{6,18},{7,19},{8,28},{9,... | collective-permute-start | bytes 159752 | tf_op jit(solution)/shard_map/ppermute | solution.py:348
  8.9 3.3 %collective-permute-done.2 = f32[104,128]{1,0:T(8,128)S(1)} collective-permute-done((f32[104,128]{1,0:T(8,128)S(1)}, f32[104,128]{1,0:T(8,128)S(1)}, u32[]{:S(2)}, u32[]{:S(2)}) %collective-permute-start.2) | collective-permute-done | bytes 53280 | tf_op jit(solution)/shard_map/ppermute | solution.py:348
  12.2 0.5 %collective-permute-start.3 = (f32[104,128]{1,0:T(8,128)S(1)}, f32[104,128]{1,0:T(8,128)S(1)}, u32[]{:S(2)}, u32[]{:S(2)}) collective-permute-start(f32[104,128]{1,0:T(8,128)S(1)} %add.17), channel_id=1, source_target_pairs={{0,5},{1,4},{2,7},{3,6},{4,1},{5,0},{6,3},{7,2},{8,13},{9,12},{10,... | collective-permute-start | bytes 159752 | tf_op jit(solution)/shard_map/ppermute | solution.py:348
  12.7 3.4 %collective-permute-done.3 = f32[104,128]{1,0:T(8,128)S(1)} collective-permute-done((f32[104,128]{1,0:T(8,128)S(1)}, f32[104,128]{1,0:T(8,128)S(1)}, u32[]{:S(2)}, u32[]{:S(2)}) %collective-permute-start.3) | collective-permute-done | bytes 53280 | tf_op jit(solution)/shard_map/ppermute | solution.py:348
  16.1 0.4 %collective-permute-start.4 = (f32[104,128]{1,0:T(8,128)S(1)}, f32[104,128]{1,0:T(8,128)S(1)}, u32[]{:S(2)}, u32[]{:S(2)}) collective-permute-start(f32[104,128]{1,0:T(8,128)S(1)} %add.18), channel_id=1, source_target_pairs={{0,6},{1,7},{2,4},{3,5},{4,2},{5,3},{6,0},{7,1},{8,14},{9,15},{10,... | collective-permute-start | bytes 159752 | tf_op jit(solution)/shard_map/ppermute | solution.py:348
  16.5 5.7 %collective-permute-done.4 = f32[104,128]{1,0:T(8,128)S(1)} collective-permute-done((f32[104,128]{1,0:T(8,128)S(1)}, f32[104,128]{1,0:T(8,128)S(1)}, u32[]{:S(2)}, u32[]{:S(2)}) %collective-permute-start.4) | collective-permute-done | bytes 53280 | tf_op jit(solution)/shard_map/ppermute | solution.py:348
  22.2 0.5 %collective-permute-start.5 = (f32[104,128]{1,0:T(8,128)S(1)}, f32[104,128]{1,0:T(8,128)S(1)}, u32[]{:S(2)}, u32[]{:S(2)}) collective-permute-start(f32[104,128]{1,0:T(8,128)S(1)} %add.19.refs_0_), channel_id=1, source_target_pairs={{0,4},{1,5},{2,6},{3,7},{4,0},{5,1},{6,2},{7,3},{8,12},{9,13},{10,... | collective-permute-start | bytes 159752 | tf_op jit(solution)/shard_map/ppermute | solution.py:348
  22.7 0.9 %collective-permute-done.5.refs_1_ = f32[104,128]{1,0:T(8,128)S(1)} collective-permute-done((f32[104,128]{1,0:T(8,128)S(1)}, f32[104,128]{1,0:T(8,128)S(1)}, u32[]{:S(2)}, u32[]{:S(2)}) %collective-permute-start.5) | collective-permute-done | bytes 53280 | tf_op jit(solution)/shard_map/ppermute | solution.py:348
  23.6 5.0 %solve.1 = (f32[512]{0:T(512)}, f32[1024]{0:T(1024)}, f32[128,128]{1,0:T(8,128)}) custom-call(f32[104,128]{1,0:T(8,128)S(1)} %add.19.refs_0_, f32[104,128]{1,0:T(8,128)S(1)} %collective-permute-done.5.refs_1_), custom_call_target="tpu_custom_call" | custom-call | tf_op jit(solution)/shard_map/solve/pallas_call | solution.py:384
  (5 shorter events, 0.0 us)
Async XLA Ops:
  2.8 1.6 %collective-permute-start = (f32[104,128]{1,0:T(8,128)S(1)}, f32[104,128]{1,0:T(8,128)S(1)}, u32[]{:S(2)}, u32[]{:S(2)}) collective-permute-start(f32[104,128]{1,0:T(8,128)S(1)} %get-tuple-element.6), channel_id=1, source_target_pairs={{0,4},{1,5},{2,6},{3,7},{4,0},{5,1},{6,2},{7,3},{8,12},{9,13},{10,... | collective-permute-start | bytes 159752 | tf_op jit(solution)/shard_map/ppermute | solution.py:348
  4.4 3.9 %collective-permute-start.1 = (f32[104,128]{1,0:T(8,128)S(1)}, f32[104,128]{1,0:T(8,128)S(1)}, u32[]{:S(2)}, u32[]{:S(2)}) collective-permute-start(f32[104,128]{1,0:T(8,128)S(1)} %add.15), channel_id=1, source_target_pairs={{0,12},{1,13},{2,14},{3,15},{4,8},{5,9},{6,10},{7,11},{8,4},{9,5},... | collective-permute-start | bytes 159752 | tf_op jit(solution)/shard_map/ppermute | solution.py:348
  8.3 3.9 %collective-permute-start.2 = (f32[104,128]{1,0:T(8,128)S(1)}, f32[104,128]{1,0:T(8,128)S(1)}, u32[]{:S(2)}, u32[]{:S(2)}) collective-permute-start(f32[104,128]{1,0:T(8,128)S(1)} %add.16), channel_id=1, source_target_pairs={{0,20},{1,21},{2,22},{3,23},{4,16},{5,17},{6,18},{7,19},{8,28},{9,... | collective-permute-start | bytes 159752 | tf_op jit(solution)/shard_map/ppermute | solution.py:348
  12.2 3.9 %collective-permute-start.3 = (f32[104,128]{1,0:T(8,128)S(1)}, f32[104,128]{1,0:T(8,128)S(1)}, u32[]{:S(2)}, u32[]{:S(2)}) collective-permute-start(f32[104,128]{1,0:T(8,128)S(1)} %add.17), channel_id=1, source_target_pairs={{0,5},{1,4},{2,7},{3,6},{4,1},{5,0},{6,3},{7,2},{8,13},{9,12},{10,... | collective-permute-start | bytes 159752 | tf_op jit(solution)/shard_map/ppermute | solution.py:348
  16.1 6.1 %collective-permute-start.4 = (f32[104,128]{1,0:T(8,128)S(1)}, f32[104,128]{1,0:T(8,128)S(1)}, u32[]{:S(2)}, u32[]{:S(2)}) collective-permute-start(f32[104,128]{1,0:T(8,128)S(1)} %add.18), channel_id=1, source_target_pairs={{0,6},{1,7},{2,4},{3,5},{4,2},{5,3},{6,0},{7,1},{8,14},{9,15},{10,... | collective-permute-start | bytes 159752 | tf_op jit(solution)/shard_map/ppermute | solution.py:348
  22.2 1.3 %collective-permute-start.5 = (f32[104,128]{1,0:T(8,128)S(1)}, f32[104,128]{1,0:T(8,128)S(1)}, u32[]{:S(2)}, u32[]{:S(2)}) collective-permute-start(f32[104,128]{1,0:T(8,128)S(1)} %add.19.refs_0_), channel_id=1, source_target_pairs={{0,4},{1,5},{2,6},{3,7},{4,0},{5,1},{6,2},{7,3},{8,12},{9,13},{10,... | collective-permute-start | bytes 159752 | tf_op jit(solution)/shard_map/ppermute | solution.py:348

commit v4 on v3

--- a/solution.py
+++ b/solution.py
@@ -375,10 +375,10 @@
         name="local_sums",
     )(*inputs)
     mine = parts[0] + swap(parts[1], n_exp, n_imp, 1, 0)
+    for bit in powers(1, n_imp):
+        mine = mine + swap(mine, n_exp, n_imp, 1, bit)
     for bit in powers(2, n_exp):
         mine = mine + swap(mine, n_exp, n_imp, bit | 1, 0)
-    for bit in powers(1, n_imp):
-        mine = mine + swap(mine, n_exp, n_imp, 1, bit)
     shares = (mine, swap(mine, n_exp, n_imp, 1, 0))
     high = 16
     a, b, g = pl.pallas_call(

time: 28.7 us -> 29.2 us (1.017)
  the two profiles are of different devices: /device:TPU:29 before, /device:TPU:0 now
where the time goes in v4:
time: 29.2 us; the launch traced here: 29 us
  starting transfers between devices  11.1 us (38%)
  waiting for transfers between devices  10 us (34%)
  Pallas kernels  7.16 us (25%)
  between operations  0.65 us (2%)
    ppermute x6, starting transfers between devices, swap(): return lax.ppermute(x, ('exp', 'imp'), pairs)  11.1 us
    ppermute x6, waiting for transfers between devices, swap(): return lax.ppermute(x, ('exp', 'imp'), pairs)  10 us
    pallas_call x1, Pallas kernels, per_device(): pl.pallas_call(functools.partial(solve_kernel, lay), out_shape=(jax.Shape...  4.98 us
    pallas_call x1, Pallas kernels, per_device(): pl.pallas_call(functools.partial(local_kernel, lay, slots), out_shape=[ja...  2.18 us
  transfers between devices with their start and end apart: 6, of which 6 were waited for; matrix products, arithmetic and copies ran while one was open for 0% of the time, Pallas kernels for 0%

profile of v4, /device:TPU:0, one launch (start us, length us, event | category | flops | bytes accessed | tf_op | source)
XLA Modules:
  0.0 29.0 jit_solution(8090397347447227093)
XLA Ops:
  0.6 2.2 %local_sums.1 = (f32[104,128]{1,0:T(8,128)S(1)}, f32[104,128]{1,0:T(8,128)S(1)}) custom-call(bf16[4,256,256]{2,1,0:T(8,128)(2,1)} %refs_0_.1, s32[4]{0:T(128)} %bitcast.5, s32[4]{0:T(128)} %refs_2_.1, s32[2,1,256]{2,1,0:T(1,128)} %bitcast.4, s32[4,1,256]{2,1,0:T(1,128)} %bitcast.3), custom_call_target="tpu_custom_call" | custom-call | tf_op jit(solution)/shard_map/local_sums/pallas_call | solution.py:366
  2.8 0.5 %collective-permute-start = (f32[104,128]{1,0:T(8,128)S(1)}, f32[104,128]{1,0:T(8,128)S(1)}, u32[]{:S(2)}, u32[]{:S(2)}) collective-permute-start(f32[104,128]{1,0:T(8,128)S(1)} %get-tuple-element.6), channel_id=1, source_target_pairs={{0,4},{1,5},{2,6},{3,7},{4,0},{5,1},{6,2},{7,3},{8,12},{9,13},{10,... | collective-permute-start | bytes 159752 | tf_op jit(solution)/shard_map/ppermute | solution.py:348
  3.3 0.9 %collective-permute-done = f32[104,128]{1,0:T(8,128)S(1)} collective-permute-done((f32[104,128]{1,0:T(8,128)S(1)}, f32[104,128]{1,0:T(8,128)S(1)}, u32[]{:S(2)}, u32[]{:S(2)}) %collective-permute-start) | collective-permute-done | bytes 53280 | tf_op jit(solution)/shard_map/ppermute | solution.py:348
  4.2 2.7 %collective-permute-start.1 = (f32[104,128]{1,0:T(8,128)S(1)}, f32[104,128]{1,0:T(8,128)S(1)}, u32[]{:S(2)}, u32[]{:S(2)}) collective-permute-start(f32[104,128]{1,0:T(8,128)S(1)} %add.15), channel_id=1, source_target_pairs={{0,5},{1,4},{2,7},{3,6},{4,1},{5,0},{6,3},{7,2},{8,13},{9,12},{10,... | collective-permute-start | bytes 159752 | tf_op jit(solution)/shard_map/ppermute | solution.py:348
  6.9 1.9 %collective-permute-done.1 = f32[104,128]{1,0:T(8,128)S(1)} collective-permute-done((f32[104,128]{1,0:T(8,128)S(1)}, f32[104,128]{1,0:T(8,128)S(1)}, u32[]{:S(2)}, u32[]{:S(2)}) %collective-permute-start.1) | collective-permute-done | bytes 53280 | tf_op jit(solution)/shard_map/ppermute | solution.py:348
  8.9 3.0 %collective-permute-start.2 = (f32[104,128]{1,0:T(8,128)S(1)}, f32[104,128]{1,0:T(8,128)S(1)}, u32[]{:S(2)}, u32[]{:S(2)}) collective-permute-start(f32[104,128]{1,0:T(8,128)S(1)} %add.16), channel_id=1, source_target_pairs={{0,6},{1,7},{2,4},{3,5},{4,2},{5,3},{6,0},{7,1},{8,14},{9,15},{10,... | collective-permute-start | bytes 159752 | tf_op jit(solution)/shard_map/ppermute | solution.py:348
  11.9 1.9 %collective-permute-done.2 = f32[104,128]{1,0:T(8,128)S(1)} collective-permute-done((f32[104,128]{1,0:T(8,128)S(1)}, f32[104,128]{1,0:T(8,128)S(1)}, u32[]{:S(2)}, u32[]{:S(2)}) %collective-permute-start.2) | collective-permute-done | bytes 53280 | tf_op jit(solution)/shard_map/ppermute | solution.py:348
  13.8 2.9 %collective-permute-start.3 = (f32[104,128]{1,0:T(8,128)S(1)}, f32[104,128]{1,0:T(8,128)S(1)}, u32[]{:S(2)}, u32[]{:S(2)}) collective-permute-start(f32[104,128]{1,0:T(8,128)S(1)} %add.17), channel_id=1, source_target_pairs={{0,12},{1,13},{2,14},{3,15},{4,8},{5,9},{6,10},{7,11},{8,4},{9,5},... | collective-permute-start | bytes 159752 | tf_op jit(solution)/shard_map/ppermute | solution.py:348
  16.7 1.8 %collective-permute-done.3 = f32[104,128]{1,0:T(8,128)S(1)} collective-permute-done((f32[104,128]{1,0:T(8,128)S(1)}, f32[104,128]{1,0:T(8,128)S(1)}, u32[]{:S(2)}, u32[]{:S(2)}) %collective-permute-start.3) | collective-permute-done | bytes 53280 | tf_op jit(solution)/shard_map/ppermute | solution.py:348
  18.5 1.8 %collective-permute-start.4 = (f32[104,128]{1,0:T(8,128)S(1)}, f32[104,128]{1,0:T(8,128)S(1)}, u32[]{:S(2)}, u32[]{:S(2)}) collective-permute-start(f32[104,128]{1,0:T(8,128)S(1)} %add.18), channel_id=1, source_target_pairs={{0,20},{1,21},{2,22},{3,23},{4,16},{5,17},{6,18},{7,19},{8,28},{9,... | collective-permute-start | bytes 159752 | tf_op jit(solution)/shard_map/ppermute | solution.py:348
  20.4 2.3 %collective-permute-done.4 = f32[104,128]{1,0:T(8,128)S(1)} collective-permute-done((f32[104,128]{1,0:T(8,128)S(1)}, f32[104,128]{1,0:T(8,128)S(1)}, u32[]{:S(2)}, u32[]{:S(2)}) %collective-permute-start.4) | collective-permute-done | bytes 53280 | tf_op jit(solution)/shard_map/ppermute | solution.py:348
  22.7 0.2 collective-permute-start.5
  22.9 1.1 %collective-permute-done.5.refs_1_ = f32[104,128]{1,0:T(8,128)S(1)} collective-permute-done((f32[104,128]{1,0:T(8,128)S(1)}, f32[104,128]{1,0:T(8,128)S(1)}, u32[]{:S(2)}, u32[]{:S(2)}) %collective-permute-start.5) | collective-permute-done | bytes 53280 | tf_op jit(solution)/shard_map/ppermute | solution.py:348
  24.0 5.0 %solve.1 = (f32[512]{0:T(512)}, f32[1024]{0:T(1024)}, f32[128,128]{1,0:T(8,128)}) custom-call(f32[104,128]{1,0:T(8,128)S(1)} %add.19.refs_0_, f32[104,128]{1,0:T(8,128)S(1)} %collective-permute-done.5.refs_1_), custom_call_target="tpu_custom_call" | custom-call | tf_op jit(solution)/shard_map/solve/pallas_call | solution.py:384
  (5 shorter events, 0.0 us)
Async XLA Ops:
  2.8 1.4 %collective-permute-start = (f32[104,128]{1,0:T(8,128)S(1)}, f32[104,128]{1,0:T(8,128)S(1)}, u32[]{:S(2)}, u32[]{:S(2)}) collective-permute-start(f32[104,128]{1,0:T(8,128)S(1)} %get-tuple-element.6), channel_id=1, source_target_pairs={{0,4},{1,5},{2,6},{3,7},{4,0},{5,1},{6,2},{7,3},{8,12},{9,13},{10,... | collective-permute-start | bytes 159752 | tf_op jit(solution)/shard_map/ppermute | solution.py:348
  4.2 4.6 %collective-permute-start.1 = (f32[104,128]{1,0:T(8,128)S(1)}, f32[104,128]{1,0:T(8,128)S(1)}, u32[]{:S(2)}, u32[]{:S(2)}) collective-permute-start(f32[104,128]{1,0:T(8,128)S(1)} %add.15), channel_id=1, source_target_pairs={{0,5},{1,4},{2,7},{3,6},{4,1},{5,0},{6,3},{7,2},{8,13},{9,12},{10,... | collective-permute-start | bytes 159752 | tf_op jit(solution)/shard_map/ppermute | solution.py:348
  8.9 4.9 %collective-permute-start.2 = (f32[104,128]{1,0:T(8,128)S(1)}, f32[104,128]{1,0:T(8,128)S(1)}, u32[]{:S(2)}, u32[]{:S(2)}) collective-permute-start(f32[104,128]{1,0:T(8,128)S(1)} %add.16), channel_id=1, source_target_pairs={{0,6},{1,7},{2,4},{3,5},{4,2},{5,3},{6,0},{7,1},{8,14},{9,15},{10,... | collective-permute-start | bytes 159752 | tf_op jit(solution)/shard_map/ppermute | solution.py:348
  13.8 4.7 %collective-permute-start.3 = (f32[104,128]{1,0:T(8,128)S(1)}, f32[104,128]{1,0:T(8,128)S(1)}, u32[]{:S(2)}, u32[]{:S(2)}) collective-permute-start(f32[104,128]{1,0:T(8,128)S(1)} %add.17), channel_id=1, source_target_pairs={{0,12},{1,13},{2,14},{3,15},{4,8},{5,9},{6,10},{7,11},{8,4},{9,5},... | collective-permute-start | bytes 159752 | tf_op jit(solution)/shard_map/ppermute | solution.py:348
  18.5 4.2 %collective-permute-start.4 = (f32[104,128]{1,0:T(8,128)S(1)}, f32[104,128]{1,0:T(8,128)S(1)}, u32[]{:S(2)}, u32[]{:S(2)}) collective-permute-start(f32[104,128]{1,0:T(8,128)S(1)} %add.18), channel_id=1, source_target_pairs={{0,20},{1,21},{2,22},{3,23},{4,16},{5,17},{6,18},{7,19},{8,28},{9,... | collective-permute-start | bytes 159752 | tf_op jit(solution)/shard_map/ppermute | solution.py:348
  22.7 1.3 %collective-permute-start.5 = (f32[104,128]{1,0:T(8,128)S(1)}, f32[104,128]{1,0:T(8,128)S(1)}, u32[]{:S(2)}, u32[]{:S(2)}) collective-permute-start(f32[104,128]{1,0:T(8,128)S(1)} %add.19.refs_0_), channel_id=1, source_target_pairs={{0,4},{1,5},{2,6},{3,7},{4,0},{5,1},{6,2},{7,3},{8,12},{9,13},{10,... | collective-permute-start | bytes 159752 | tf_op jit(solution)/shard_map/ppermute | solution.py:348
